TPU v7x, 32 devices: a whole 2x2x4 slice. The times are simulated.
32 devices in a mesh: group: 2 (over y), swap: 8 (over z, x), image: 2 (over core).
Axes of the slice: x: 2, y: 2, z: 4, core: 2. Of those that a mesh axis runs over, the one named last changes fastest.
Arguments:
- images_in: bfloat16 [16, 1536, 4096], P(('group', 'image'), 'swap'), parts along dimension 0, may hold values from -6 to 6
- kernel: bfloat16 [1536, 49], P('swap'), may hold values from -1.75 to 1.75
- conv_bias: float32 [1536], P('swap'), may hold values from -1 to 1
- norm_gain: float32 [1536], replicated, may hold values from 0.1 to 1.9
- norm_shift: float32 [1536], replicated, may hold values from -0.5 to 0.5
- fp8_weight: bfloat16 [1536, 6144], P('swap', 'image'), may hold values from -1.875 to 1.875, as said below
- block_scale: int32 [1536, 48], P('swap', 'image'), may hold values from -7 to -5
- adapter_a: bfloat16 [1536, 32], replicated, may hold values from -0.15625 to 0.15625
- adapter_b: bfloat16 [32, 6144], P(None, 'image'), may hold values from -0.25 to 0.25
- cotangent: bfloat16 [16, 4096, 6144], P('group', 'swap', 'image'), parts along dimension 0, may hold values from -0.05 to 0.05
Outputs:
- grad_a: float32 [3072, 32], P('group'), parts along dimension 0
- grad_b: float32 [64, 6144], P('group', 'image'), parts along dimension 0
There are 2 independent parts, one for each index of `group`. A program takes and returns all parts, laid end to end along the dimension named above; an argument that names none is the same for every part. Nothing has to cross between parts.
Inputs may be any that keep to these rules, and one draw needn't show every extreme that they name: `fp8_weight`: each entry is a value of the E4M3 format: a sign times 2 to an integer power times 1 + k / 8 for an integer k of 0 to 7. `block_scale`: the entry at [c, j] is the exponent of the scale of hidden units 128 * j to 128 * j + 127 of weight row c.
All inputs are finite; a program needn't handle non-finite values.
Results may differ from a plain program's by a relative error of at most 0.00055.
The roundings to bfloat16 on the way count: a program that leaves them out, or rounds other values in their place, can miss the bound.
Values may be sent and summed in bfloat16 or wider, within the bound.
No kernel may reach another device: no remote copies, remote signals or barrier semaphores. Data moves between devices by JAX's collectives and lax.ppermute only.
A program may use at most 192 MiB of HBM per device.

v0:
```python
import jax
import jax.numpy as jnp
from jax import lax
from jax.sharding import PartitionSpec as P

KS = 7
W = 64


adapter_scale = 2.0
norm_eps = 1e-06


def power_table(scales):
    factor = jnp.zeros(scales.shape, jnp.float32)
    for exponent in range(-12, 4):
        factor = factor + jnp.where(
            scales == exponent, jnp.float32(2.0**exponent), jnp.float32(0.0)
        )
    return factor


def decode(weight, scales):
    row_count = weight.shape[0]
    groups = scales.shape[1]
    blocks = (
        weight.reshape(row_count, groups, -1).astype(jnp.float32) * power_table(scales)[:, :, None]
    )
    return blocks.reshape(row_count, -1).astype(jnp.bfloat16)


def gelu_slope(pre_act):
    cumulative = 0.5 * (1.0 + jax.scipy.special.erf(pre_act * 0.7071067811865476))
    density = jnp.exp(-0.5 * pre_act * pre_act) * 0.3989422804014327
    return cumulative + pre_act * density


def depthwise(images, kernel, conv_bias, map_width):
    batch, channels, pixels = images.shape
    maps = images.reshape(batch, channels, pixels // map_width, map_width)
    taps = kernel.reshape(channels, 1, KS, KS)
    half_span = KS // 2
    summed = lax.conv_general_dilated(
        maps,
        taps,
        (1, 1),
        ((half_span, half_span), (half_span, half_span)),
        dimension_numbers=("NCHW", "OIHW", "NCHW"),
        feature_group_count=channels,
        preferred_element_type=jnp.float32,
    )
    summed = summed.reshape(batch, channels, pixels)
    return summed + conv_bias[None, :, None]


def shards(
    images_in,
    kernel,
    conv_bias,
    norm_gain,
    norm_shift,
    fp8_weight,
    block_scale,
    adapter_a,
    adapter_b,
    cotangent,
):
    conv = depthwise(images_in, kernel, conv_bias, W).astype(jnp.bfloat16)
    values = lax.all_to_all(conv, "swap", split_axis=2, concat_axis=1, tiled=True).astype(
        jnp.float32
    )
    average = jnp.mean(values, axis=1, keepdims=True)
    centred = values - average
    variance = jnp.mean(centred * centred, axis=1, keepdims=True)
    scaled = (
        centred * lax.rsqrt(variance + norm_eps) * norm_gain[None, :, None]
        + norm_shift[None, :, None]
    )
    normed = jnp.swapaxes(scaled, 1, 2).astype(jnp.bfloat16)
    own_rows = normed.reshape(-1, normed.shape[2])
    tokens = lax.all_gather(own_rows, "image", axis=0, tiled=True)
    zero_start = jnp.zeros((tokens.shape[0], fp8_weight.shape[1]), jnp.float32)
    local_weight = decode(fp8_weight, block_scale)
    shard_rows = lax.all_gather(local_weight, "swap", axis=0, tiled=True)
    columns = lax.slice_in_dim(tokens, 0, shard_rows.shape[0], axis=1)
    frozen = zero_start + jnp.dot(columns, shard_rows, preferred_element_type=jnp.float32)
    low_rank = jnp.dot(tokens, adapter_a, preferred_element_type=jnp.float32).astype(jnp.bfloat16)
    pre_act = frozen + adapter_scale * jnp.dot(
        low_rank, adapter_b, preferred_element_type=jnp.float32
    )
    upstream = cotangent.reshape(-1, cotangent.shape[2])
    grad_pre = (upstream.astype(jnp.float32) * gelu_slope(pre_act)).astype(jnp.bfloat16)
    grad_b_local = adapter_scale * jnp.dot(low_rank.T, grad_pre, preferred_element_type=jnp.float32)
    partial_back = jnp.dot(grad_pre, adapter_b.T, preferred_element_type=jnp.float32)
    contract = (((0,), (0,)), ((), ()))
    tokens_wide = tokens.astype(jnp.float32)
    summed_back = lax.psum(partial_back, "image")
    grad_a_local = adapter_scale * lax.dot_general(
        tokens_wide,
        summed_back,
        contract,
        precision=lax.Precision.HIGHEST,
        preferred_element_type=jnp.float32,
    )
    grad_a, grad_b = lax.psum((grad_a_local, grad_b_local), "swap")
    return (grad_a, grad_b)


def solution(mesh):
    placed = (
        P(("group", "image"), "swap", None),
        P("swap", None),
        P("swap"),
        P(),
        P(),
        P("swap", "image"),
        P("swap", "image"),
        P(),
        P(None, "image"),
        P("group", "swap", "image"),
    )
    return jax.shard_map(
        shards,
        mesh=mesh,
        in_specs=placed,
        out_specs=(P("group", None), P("group", "image")),
        check_vma=False,
    )
```

profile of v0, /device:TPU:0, one launch (start us, length us, event | category | flops | bytes accessed | tf_op | source)
XLA Modules:
  0.0 838.4 jit_solution(14557225846373415734)
XLA Ops:
  8.1 10.6 %copy.43 = bf16[4,192,4096]{1,2,0:T(8,128)(2,1)} copy(bf16[4,192,4096]{2,1,0:T(8,128)(2,1)} %param.10) | data formatting | bytes 12582912 | tf_op args[0]
  18.7 11.5 %copy.54 = bf16[192,64,4,64]{0,1,3,2:T(8,128)(2,1)} copy(bf16[192,64,4,64]{0,3,1,2:T(8,128)(2,1)} %bitcast.75) | data formatting | bytes 12582912
  30.2 10.0 %pad.clone = bf16[192,64,4,72]{0,1,3,2:T(8,128)(2,1)} pad(bf16[192,64,4,64]{0,1,3,2:T(8,128)(2,1)} %copy.54, bf16[]{:T(256)} %constant.37), padding=0_0x0_0x0_0x3_5 | pad | bytes 13369346 | tf_op jit(solution)/shard_map/reshape | solution.py:40
  49.7 95.9 %broadcast_select_fusion = f32[64,32,9,192]{3,1,2,0:T(8,128)S(1)} fusion(pred[32,9]{0,1:T(8,128)(4,1)S(1)} %copy-done.9, bf16[192,1,7,7]{0,1,3,2:T(2,128)(2,1)S(1)} %reshape.62, bf16[192,64,4,8,15]{0,1,4,3,2:T(8,128)(2,1)S(1)} %fusion.8), kind=kOutput, calls=%fused_computation.23 | convolution fusion | flops 341065728 | bytes 25971360 | tf_op jit(solution)/shard_map/conv_general_dilated | solution.py:43
  145.6 20.1 %copy.47 = f32[64,32,9,192]{3,0,2,1:T(8,128)S(1)} copy(f32[64,32,9,192]{3,1,2,0:T(8,128)S(1)} %broadcast_select_fusion) | data formatting | bytes 28311552 | tf_op jit(solution)/shard_map/conv_general_dilated | solution.py:43
  167.8 17.9 %copy.48 = f32[4,192,64,64]{1,3,2,0:T(8,128)S(1)} copy(f32[4,192,64,64]{1,2,3,0:T(8,128)S(1)} %slice_bitcast_fusion) | data formatting | bytes 25165824 | tf_op jit(solution)/shard_map/conv_general_dilated | solution.py:43
  188.3 31.9 %copy.49 = bf16[4,192,4096]{1,0,2:T(4,128)(2,1)S(1)} copy(bf16[4,192,4096]{1,2,0:T(8,128)(2,1)S(1)} %fusion.7) | data formatting | bytes 12582912 | tf_op jit(solution)/shard_map/convert_element_type | solution.py:68
  220.1 190.2 %all_to_all.4 = bf16[4,192,4096]{1,0,2:T(4,128)(2,1)} all-to-all(bf16[4,192,4096]{1,0,2:T(4,128)(2,1)S(1)} %copy.49), channel_id=1, replica_groups=mesh['group'=2,'swap'=8,'image'=2] {'swap'}, dimensions={2} | all-to-all | bytes 12582912 | tf_op jit(solution)/shard_map/all_to_all | solution.py:69
  410.3 13.5 %copy.50 = bf16[4,192,4096]{2,1,0:T(8,128)(2,1)} copy(bf16[4,192,4096]{1,0,2:T(4,128)(2,1)} %all_to_all.4) | data formatting | bytes 12582912 | tf_op jit(solution)/shard_map/all_to_all | solution.py:69
  423.8 9.1 %copy.55 = f32[96,8,8,512]{3,2,1,0:T(8,128)S(1)} copy(bf16[96,8,8,512]{3,1,2,0:T(8,128)(2,1)} %bitcast.77) | data formatting | bytes 18874368
  439.0 10.6 %bitcast_bitcast_fusion = f32[4,8,192,512]{3,1,2,0:T(8,128)} fusion(f32[4,192,8,512]{3,2,1,0:T(8,128)} %bitcast.71), kind=kLoop, calls=%fused_computation.16 | loop fusion | bytes 25165824 | tf_op jit(solution)/shard_map/convert_element_type | solution.py:69
  449.7 16.6 %copy.51 = f32[4,8,192,512]{3,2,1,0:T(8,128)} copy(f32[4,8,192,512]{3,1,2,0:T(8,128)} %bitcast_bitcast_fusion) | data formatting | bytes 25165824 | tf_op jit(solution)/shard_map/convert_element_type | solution.py:69
  466.2 9.0 %fusion.15 = bf16[4,1536,512]{2,1,0:T(8,128)(2,1)} fusion(f32[4,8,192,512]{3,2,1,0:T(8,128)} %copy.51, f32[1536]{0:T(1024)S(1)} %copy-done.6, f32[1536]{0:T(1024)S(1)} %copy-done.7, f32[4,512]{1,0:T(4,128)S(1)} %add_rsqrt_fusion, f32[4,512]{1,0:T(4,128)S(1)} %broadcast_multiply_fusion), kind=kLoop, calls=%fused_computation.21 | loop fusion | flops 15728640 | bytes 18903040 | tf_op jit(solution)/shard_map/convert_element_type | solution.py:79
  475.2 8.7 %copy.52 = bf16[4,512,1536]{2,1,0:T(8,128)(2,1)} copy(bf16[4,512,1536]{1,2,0:T(8,128)(2,1)} %bitcast.78) | data formatting | bytes 12582912 | tf_op jit(solution)/shard_map/convert_element_type | solution.py:79
  486.5 21.5 %all-gather.3.cloned.1.call-done = bf16[4096,1536]{1,0:T(8,128)(2,1)} async-done(((bf16[2048,1536]{1,0:T(8,128)(2,1)}), bf16[4096,1536]{1,0:T(8,128)(2,1)}) %all-gather.3.cloned.1.call-update) | async-done | bytes 12582928 | tf_op jit(solution)/shard_map/all_gather | solution.py:81
  508.0 8.3 convolution_convert_fusion
  516.4 20.3 %fusion.20 = f32[4096,3072]{1,0:T(8,128)} fusion(bf16[4096,32]{0,1:T(8,128)(2,1)S(1)} %convolution_convert_fusion, bf16[32,3072]{1,0:T(8,128)(2,1)S(1)} %copy-done), kind=kOutput, calls=%fused_computation.33 | convolution fusion | flops 805306368 | bytes 50790400 | tf_op jit(solution)/shard_map/dot_general | solution.py:88
  536.7 112.8 %all-gather.5.cloned.1.call-done = bf16[1536,3072]{1,0:T(8,128)(2,1)} async-done(((bf16[192,3072]{1,0:T(8,128)(2,1)}), bf16[1536,3072]{1,0:T(8,128)(2,1)}) %all-gather.5.cloned.1.call-update) | async-done | bytes 9437200 | tf_op jit(solution)/shard_map/all_gather | solution.py:84
  649.5 64.7 %fusion.5 = bf16[4096,3072]{1,0:T(8,128)(2,1)} fusion(bf16[4096,3072]{1,0:T(8,128)(2,1)} %bitcast.80, f32[4096,3072]{1,0:T(8,128)} %fusion.20, bf16[4096,1536]{1,0:T(8,128)(2,1)} %all-gather.3.cloned.1.call-done, bf16[1536,3072]{1,0:T(8,128)(2,1)} %all-gather.5.cloned.1.call-done), kind=kOutput, calls=%fused_computation.6 | convolution fusion | flops 38818283520 | bytes 122683392 | tf_op jit(solution)/shard_map/dot_general | solution.py:86
  714.1 12.9 %fusion.21 = f32[4096,32]{0,1:T(8,128)} fusion(bf16[4096,3072]{1,0:T(8,128)(2,1)} %fusion.5, bf16[32,3072]{1,0:T(8,128)(2,1)S(1)} %copy-done), kind=kOutput, calls=%fused_computation.34 | convolution fusion | flops 805306368 | bytes 25886720 | tf_op jit(solution)/shard_map/dot_general | solution.py:94
  727.1 11.7 %convolution_multiply_fusion = f32[32,3072]{1,0:T(8,128)} fusion(bf16[4096,32]{0,1:T(8,128)(2,1)S(1)} %convolution_convert_fusion, bf16[4096,3072]{1,0:T(8,128)(2,1)} %fusion.5), kind=kOutput, calls=%fused_computation.25 | convolution fusion | flops 805404672 | bytes 25821184 | tf_op jit(solution)/shard_map/dot_general | solution.py:93
  738.7 5.4 all-reduce.4.cloned.1.call-done
  744.1 9.8 %convolution_multiply_fusion.1 = f32[1536,32]{0,1:T(8,128)} fusion(bf16[4096,1536]{1,0:T(8,128)(2,1)} %all-gather.3.cloned.1.call-done, f32[4096,32]{0,1:T(8,128)} %all-reduce.4.cloned.1.call-done), kind=kOutput, calls=%fused_computation.28 | convolution fusion | flops 2415968256 | bytes 13303808 | tf_op jit(solution)/shard_map/dot_general | solution.py:98
  753.9 74.4 %all-reduce.6.cloned.1.call-done = (f32[1536,32]{0,1:T(8,128)}, f32[32,3072]{1,0:T(8,128)}) async-done(((f32[1536,32]{0,1:T(8,128)}, f32[32,3072]{1,0:T(8,128)}), (f32[1536,32]{0,1:T(8,128)}, f32[32,3072]{1,0:T(8,128)})) %all-reduce.6.cloned.1.call-update) | async-done | bytes 589840 | tf_op jit(solution)/shard_map/psum | solution.py:105
  (43 shorter events, 27.1 us)
Async XLA Ops:
  7.2 509.2 %copy-start = (bf16[32,3072]{1,0:T(8,128)(2,1)S(1)}, bf16[32,3072]{1,0:T(8,128)(2,1)}, u32[]{:S(2)}) copy-start(bf16[32,3072]{1,0:T(8,128)(2,1)} %param.18) | copy-start | bytes 589828
  7.2 500.8 %all-gather.3.cloned.1.call-start = ((), (), s32[]{:S(2)}) async-start(), calls=%async_computation.1 | async-start | bytes 18874368 | tf_op jit(solution)/shard_map/all_gather | solution.py:81
  40.2 5.3 copy-start.2
  45.5 4.2 copy-start.9
  167.7 17.9 %copy-start.8 = (f32[192]{0:T(256)S(1)}, f32[192]{0:T(256)}, u32[]{:S(2)}) copy-start(f32[192]{0:T(256)} %param.12) | copy-start | bytes 2308
  432.9 4.5 copy-start.1
  449.7 16.6 %copy-start.6 = (f32[1536]{0:T(1024)S(1)}, f32[1536]{0:T(1024)}, u32[]{:S(2)}) copy-start(f32[1536]{0:T(1024)} %param.14) | copy-start | bytes 18436
  449.7 16.6 %copy-start.7 = (f32[1536]{0:T(1024)S(1)}, f32[1536]{0:T(1024)}, u32[]{:S(2)}) copy-start(f32[1536]{0:T(1024)} %param.13) | copy-start | bytes 18436
  466.2 17.8 %copy-start.5 = (s32[192,24]{0,1:T(8,128)S(1)}, s32[192,24]{0,1:T(8,128)}, u32[]{:S(2)}) copy-start(s32[192,24]{0,1:T(8,128)} %param.16) | copy-start | bytes 55300
  466.2 18.6 %copy-start.3 = (bf16[192,3072]{1,0:T(8,128)(2,1)S(1)}, bf16[192,3072]{1,0:T(8,128)(2,1)}, u32[]{:S(2)}) copy-start(bf16[192,3072]{1,0:T(8,128)(2,1)} %param.15) | copy-start | bytes 3538948
  475.2 32.8 %copy-start.4 = (bf16[1536,32]{0,1:T(8,128)(2,1)S(1)}, bf16[1536,32]{0,1:T(8,128)(2,1)}, u32[]{:S(2)}) copy-start(bf16[1536,32]{0,1:T(8,128)(2,1)} %param.17) | copy-start | bytes 294916
  483.9 165.5 %all-gather.5.cloned.1.call-start = ((), (), s32[]{:S(2)}) async-start(), calls=%async_computation.2 | async-start | bytes 10616832 | tf_op jit(solution)/shard_map/all_gather | solution.py:84
  486.5 257.6 %all-reduce.4.cloned.1.call-start = ((), (), s32[]{:S(2)}) async-start(), calls=%async_computation.3 | async-start | bytes 1048576 | tf_op jit(solution)/shard_map/psum | solution.py:97
  727.0 101.3 %all-reduce.6.cloned.1.call-start = ((), (), s32[]{:S(2)}) async-start(), calls=%async_computation.4 | async-start | bytes 1179648 | tf_op jit(solution)/shard_map/psum | solution.py:105
Sparse Core Ops, SparseCore 0:
  484.1 23.9 all-gather.2
  510.2 139.2 all-gather.4
  727.2 16.9 all-reduce.3
  754.1 74.2 all-reduce.5
where the time goes:
time: 846 us; the launch traced here: 838 us
  matrix products  223 us (26%)
  waiting for transfers between devices  214 us (25%)
  blocking collectives  190 us (22%)
  local copies, waits for them, and re-layouts  176 us (21%)
  other arithmetic  20 us (2%)
  between operations  14.1 us (2%)
    all_to_all x1, blocking collectives, shards(): lax.all_to_all(conv, 'swap', split_axis=2, concat_axis=1, tiled=True)  190 us
    all_gather x1, waiting for transfers between devices, shards(): shard_rows = lax.all_gather(local_weight, 'swap', axis=0, tiled=True)  113 us
    conv_general_dilated x1, matrix products, depthwise(): lax.conv_general_dilated(maps, taps, (1, 1), ((half_span, half_span), (ha...  95.9 us
    psum x1, waiting for transfers between devices, shards(): grad_a, grad_b = lax.psum((grad_a_local, grad_b_local), 'swap')  74.4 us
    dot_general x1, matrix products, shards(): jnp.dot(columns, shard_rows, preferred_element_type=jnp.float32)  64.7 us
    conv_general_dilated x4, local copies, waits for them, and re-layouts, depthwise(): lax.conv_general_dilated(maps, taps, (1, 1), ((half_span, half_span), (ha...  43.4 us
    unnamed x25, local copies, waits for them, and re-layouts  40 us
    convert_element_type x1, local copies, waits for them, and re-layouts, shards(): conv = depthwise(images_in, kernel, conv_bias, W).astype(jnp.bfloat16)  31.9 us
  transfers between devices with their start and end apart: 4, of which 4 were waited for; matrix products, arithmetic and copies ran while one was open for 5% of the time, Pallas kernels for 0%

commit v1 on v0

v1 whole, which is shorter than its diff:
```python
import functools

import jax
import jax.numpy as jnp
from jax import lax
from jax.experimental import pallas as pl
from jax.experimental.pallas import tpu as pltpu
from jax.sharding import PartitionSpec as P

KS = 7
W = 64
LANES = 128
HALF = KS // 2

adapter_scale = 2.0
norm_eps = 1e-06

TAIL_STEP = 0.275
TAIL = (0.11780931, 0.04211112, 0.33393318, -0.33099448, 0.45199936, -0.11485849)
DENSITY = 0.3989422804014327
VMEM_LIMIT = 56 * 1024 * 1024


def power_table(scales):
    factor = jnp.zeros(scales.shape, jnp.float32)
    for exponent in range(-12, 4):
        factor = factor + jnp.where(
            scales == exponent, jnp.float32(2.0**exponent), jnp.float32(0.0)
        )
    return factor


def decode(weight, scales):
    row_count = weight.shape[0]
    groups = scales.shape[1]
    blocks = (
        weight.reshape(row_count, groups, -1).astype(jnp.float32) * power_table(scales)[:, :, None]
    )
    return blocks.reshape(row_count, -1).astype(jnp.bfloat16)


def params(**more):
    return pltpu.CompilerParams(vmem_limit_bytes=VMEM_LIMIT, **more)


def conv_body(where, image, taps, bias, *rest, parts, tile_rows):
    outs, (padded, coefs, sums) = rest[:parts], rest[parts:]
    channels, pixels = image.shape[1:]
    tiles = pixels // LANES
    span = pixels // parts
    margin = 2 * LANES
    padded[:, :margin] = jnp.zeros((channels, margin), jnp.float32)
    padded[:, margin + pixels :] = jnp.zeros((channels, margin), jnp.float32)
    padded[:, margin : margin + pixels] = image[0].astype(jnp.float32)
    wide = taps[...].astype(jnp.float32)
    for tap in range(KS * KS):
        coefs[tap] = jnp.broadcast_to(wide[:, tap : tap + 1], (channels, LANES))
    lane = lax.broadcasted_iota(jnp.int32, (8, LANES), 1)
    column = lane % W
    first = lane < W

    def some(step, carry):
        group, block = step // (tiles // tile_rows), step % (tiles // tile_rows)
        rows = pl.ds(pl.multiple_of(group * 8, 8), 8)
        start = block * (tile_rows * LANES)
        count = tile_rows + 4
        raw = [
            padded[rows, pl.ds(pl.multiple_of(start + i * LANES, LANES), LANES)]
            for i in range(count)
        ]
        base = jnp.broadcast_to(bias[rows, :], (8, LANES))
        total = [base] * tile_rows
        for b in range(KS):
            shift = b - HALF
            if shift:
                moved = column + shift
                inside = (moved >= 0) & (moved < W)
                lined = [
                    jnp.where(inside, pltpu.roll(tile, (-shift) % LANES, 1), 0.0) for tile in raw
                ]
            else:
                lined = raw
            for row_step in (-2, 0, 2):
                coef = coefs[(row_step + HALF) * KS + b, rows, :]
                for j in range(tile_rows):
                    total[j] = total[j] + lined[j + 2 + row_step // 2] * coef
            turned = [pltpu.roll(tile, W, 1) for tile in lined]
            between = [jnp.where(first, turned[i], turned[i + 1]) for i in range(count - 1)]
            for row_step in (-3, -1, 1, 3):
                coef = coefs[(row_step + HALF) * KS + b, rows, :]
                for j in range(tile_rows):
                    total[j] = total[j] + between[j + 2 + (row_step - 1) // 2] * coef
        for j in range(tile_rows):
            sums[rows, pl.ds(pl.multiple_of(start + j * LANES, LANES), LANES)] = total[j]
        return carry

    lax.fori_loop(0, (channels // 8) * (tiles // tile_rows), some, 0)
    for k in range(parts):
        origin = pl.multiple_of(lax.bitwise_xor(where[0], k) * span, LANES)
        outs[k][...] = sums[:, pl.ds(origin, span)].astype(jnp.bfloat16)


def conv_image(index, place, images, kernel, conv_bias, parts):
    _, channels, pixels = images.shape
    rows = 16
    tiles = pixels // LANES
    tile_rows = 16 if tiles % 16 == 0 else 1
    span = pixels // parts
    return pl.pallas_call(
        functools.partial(conv_body, parts=parts, tile_rows=tile_rows),
        grid_spec=pltpu.PrefetchScalarGridSpec(
            num_scalar_prefetch=1,
            grid=(channels // rows,),
            in_specs=[
                pl.BlockSpec((1, rows, pixels), lambda c, place: (index, c, 0)),
                pl.BlockSpec((rows, KS * KS), lambda c, place: (c, 0)),
                pl.BlockSpec((rows, 1), lambda c, place: (c, 0)),
            ],
            out_specs=[pl.BlockSpec((rows, span), lambda c, place: (c, 0))] * parts,
            scratch_shapes=[
                pltpu.VMEM((rows, pixels + 4 * LANES), jnp.float32),
                pltpu.VMEM((KS * KS, rows, LANES), jnp.float32),
                pltpu.VMEM((rows, pixels), jnp.float32),
            ],
        ),
        out_shape=[jax.ShapeDtypeStruct((channels, span), jnp.bfloat16)] * parts,
        compiler_params=params(),
        name=f"conv_{index}",
    )(place, images, kernel, conv_bias)


def norm_body(where, *refs, parts):
    pieces, (gain, shift, out, values) = refs[:parts], refs[parts:]
    rows = pieces[0].shape[0]
    for k in range(parts):
        origin = pl.multiple_of(lax.bitwise_xor(where[0], k) * rows, 16)
        values[pl.ds(origin, rows), :] = pieces[k][...].astype(jnp.float32)
    channels = values.shape[0]
    average = jnp.sum(values[...], axis=0, keepdims=True) * (1.0 / channels)
    centred = values[...] - average
    variance = jnp.sum(centred * centred, axis=0, keepdims=True) * (1.0 / channels)
    scaled = centred * lax.rsqrt(variance + norm_eps) * gain[...] + shift[...]
    out[...] = scaled.astype(jnp.bfloat16).T


def norm_image(index, place, pieces, gain, shift):
    parts = len(pieces)
    rows, span = pieces[0].shape
    channels = rows * parts
    width = LANES
    return pl.pallas_call(
        functools.partial(norm_body, parts=parts),
        grid_spec=pltpu.PrefetchScalarGridSpec(
            num_scalar_prefetch=1,
            grid=(span // width,),
            in_specs=[pl.BlockSpec((rows, width), lambda p, place: (0, p))] * parts
            + [pl.BlockSpec((channels, 1), lambda p, place: (0, 0))] * 2,
            out_specs=pl.BlockSpec((width, channels), lambda p, place: (p, 0)),
            scratch_shapes=[pltpu.VMEM((channels, width), jnp.float32)],
        ),
        out_shape=jax.ShapeDtypeStruct((span, channels), jnp.bfloat16),
        compiler_params=params(),
        name=f"norm_{index}",
    )(place, *pieces, gain, shift)


def gelu_slope(x):
    size = jnp.abs(x)
    t = 1.0 / (1.0 + TAIL_STEP * size)
    tail = TAIL[-1]
    for coefficient in TAIL[-2::-1]:
        tail = tail * t + coefficient
    fall = jnp.exp(-0.5 * (x * x)) * (DENSITY * size - tail * t)
    return jnp.where(x >= 0, 1.0 + fall, -fall)


def main_body(where, own, other, weight, down, up, cot_own, cot_other, grad_a, grad_b, low, low_t, back, pre, *, step):
    f = pl.program_id(0)
    span = own.shape[0]
    sides = ((own, cot_own, 0), (other, cot_other, span))

    @pl.when(f == 0)
    def first():
        for tokens, _, base in sides:
            product = jnp.dot(tokens[...], down[...], preferred_element_type=jnp.float32)
            rounded = product.astype(jnp.bfloat16).astype(jnp.float32) * adapter_scale
            low[base : base + span, :] = rounded.astype(jnp.bfloat16)
            low_t[:, base : base + span] = rounded.T.astype(jnp.bfloat16)
        back[...] = jnp.zeros_like(back)

    blocks = [
        (tokens, cot, start, base + start)
        for tokens, cot, base in sides
        for start in range(0, span, step)
    ]
    grad_b_total = None

    def project(n):
        tokens, _, start, place = blocks[n]
        pre[n % 2] = jnp.dot(
            tokens[start : start + step, :], weight[...], preferred_element_type=jnp.float32
        ) + jnp.dot(low[place : place + step, :], up[...], preferred_element_type=jnp.float32)

    project(0)
    for n, (_, cot, start, place) in enumerate(blocks):
        if n + 1 < len(blocks):
            project(n + 1)
        slope = gelu_slope(pre[n % 2])
        grad_pre = (cot[0, start : start + step, :].astype(jnp.float32) * slope).astype(jnp.bfloat16)
        product = jnp.dot(
            low_t[:, place : place + step], grad_pre, preferred_element_type=jnp.float32
        )
        grad_b_total = product if grad_b_total is None else grad_b_total + product
        back[:, place : place + step] += lax.dot_general(
            up[...], grad_pre, (((1,), (1,)), ((), ())), preferred_element_type=jnp.float32
        )
    grad_b[...] = grad_b_total

    @pl.when(f == pl.num_programs(0) - 1)
    def last():
        rank = back.shape[0]
        total = None
        for tokens, _, base in sides:
            wide = back[:, base : base + span] * adapter_scale
            high = wide.astype(jnp.bfloat16)
            rest = (wide - high.astype(jnp.float32)).astype(jnp.bfloat16)
            both = jnp.concatenate([high, rest], axis=0)
            product = jnp.dot(both, tokens[...], preferred_element_type=jnp.float32)
            total = product if total is None else total + product
        grad_a[...] = total[:rank] + total[rank:]


def main_chunk(index, place, own, other, weight, down, up, cotangent):
    span, channels = own.shape
    hidden = weight.shape[1]
    rank = down.shape[1]
    half = cotangent.shape[0] // 2
    width = 512 if hidden % 512 == 0 else LANES
    step = 256 if span % 256 == 0 else span
    return pl.pallas_call(
        functools.partial(main_body, step=step),
        grid_spec=pltpu.PrefetchScalarGridSpec(
            num_scalar_prefetch=1,
            grid=(hidden // width,),
            in_specs=[
                pl.BlockSpec((span, channels), lambda f, place: (0, 0)),
                pl.BlockSpec((span, channels), lambda f, place: (0, 0)),
                pl.BlockSpec((channels, width), lambda f, place: (0, f)),
                pl.BlockSpec((channels, rank), lambda f, place: (0, 0)),
                pl.BlockSpec((rank, width), lambda f, place: (0, f)),
                pl.BlockSpec((1, span, width), lambda f, place: (place[1] * half + index, 0, f)),
                pl.BlockSpec((1, span, width), lambda f, place: ((1 - place[1]) * half + index, 0, f)),
            ],
            out_specs=[
                pl.BlockSpec((rank, channels), lambda f, place: (0, 0)),
                pl.BlockSpec((rank, width), lambda f, place: (0, f)),
            ],
            scratch_shapes=[
                pltpu.VMEM((2 * span, rank), jnp.bfloat16),
                pltpu.VMEM((rank, 2 * span), jnp.bfloat16),
                pltpu.VMEM((rank, 2 * span), jnp.float32),
                pltpu.VMEM((2, step, width), jnp.float32),
            ],
        ),
        out_shape=[
            jax.ShapeDtypeStruct((rank, channels), jnp.float32),
            jax.ShapeDtypeStruct((rank, hidden), jnp.float32),
        ],
        compiler_params=params(),
        name=f"main_{index}",
    )(place, own, other, weight, down, up, cotangent, cotangent)


def across(parts, k):
    return [(s, s ^ k) for s in range(parts)]


def total_over_swap(parts, me, share):
    mine = lax.dynamic_index_in_dim(share, me, 0, keepdims=False)
    got = [
        lax.ppermute(
            lax.dynamic_index_in_dim(share, lax.bitwise_xor(me, k), 0, keepdims=False),
            "swap",
            across(parts, k),
        )
        for k in range(parts - 1, 0, -1)
    ]
    for piece in got:
        mine = mine + piece
    whole = jnp.zeros(share.shape, share.dtype)
    whole = lax.dynamic_update_index_in_dim(whole, mine, me, 0)
    for k in range(parts - 1, 0, -1):
        piece = lax.ppermute(mine, "swap", across(parts, k))
        whole = lax.dynamic_update_index_in_dim(whole, piece, lax.bitwise_xor(me, k), 0)
    return whole


def shards_kernels(
    parts,
    images_in,
    kernel,
    conv_bias,
    norm_gain,
    norm_shift,
    fp8_weight,
    block_scale,
    adapter_a,
    adapter_b,
    cotangent,
):
    me = lax.axis_index("swap")
    side = lax.axis_index("image")
    place = jnp.stack([me, side]).astype(jnp.int32)
    local_weight = decode(fp8_weight, block_scale)
    weight = lax.all_gather(local_weight, "swap", axis=0, tiled=True)
    bias, gain, shift = conv_bias[:, None], norm_gain[:, None], norm_shift[:, None]
    grad_a, grad_b = [], []
    for index in range(images_in.shape[0]):
        pieces = conv_image(index, place, images_in, kernel, bias, parts)
        arrived = [pieces[0]] + [
            lax.ppermute(pieces[k], "swap", across(parts, k)) for k in range(1, parts)
        ]
        own = norm_image(index, place, arrived, gain, shift)
        other = lax.ppermute(own, "image", [(0, 1), (1, 0)])
        one_a, one_b = main_chunk(
            index, place, own, other, weight, adapter_a, adapter_b, cotangent
        )
        grad_a.append(one_a)
        grad_b.append(one_b)
    rank = adapter_a.shape[1]
    sum_a, sum_b = sum(grad_a[1:], grad_a[0]), sum(grad_b[1:], grad_b[0])
    half = sum_a.shape[1] // 2
    halves = sum_a.reshape(rank, 2, half).swapaxes(0, 1)
    kept = lax.dynamic_index_in_dim(halves, side, 0, keepdims=False)
    given = lax.dynamic_index_in_dim(halves, 1 - side, 0, keepdims=False)
    kept = kept + lax.ppermute(given, "image", [(0, 1), (1, 0)])
    joined = jnp.concatenate([kept, sum_b], axis=1)
    share = joined.reshape(rank, parts, -1).swapaxes(0, 1)
    whole = total_over_swap(parts, me, share).swapaxes(0, 1).reshape(rank, -1)
    kept, sum_b = whole[:, :half], whole[:, half:]
    given = lax.ppermute(kept, "image", [(0, 1), (1, 0)])
    low = jnp.where(side == 0, kept, given)
    high = jnp.where(side == 0, given, kept)
    return jnp.concatenate([low, high], axis=1).T, sum_b


def shards_plain(
    images_in,
    kernel,
    conv_bias,
    norm_gain,
    norm_shift,
    fp8_weight,
    block_scale,
    adapter_a,
    adapter_b,
    cotangent,
):
    batch, channels, pixels = images_in.shape
    maps = images_in.reshape(batch, channels, pixels // W, W)
    conv = lax.conv_general_dilated(
        maps,
        kernel.reshape(channels, 1, KS, KS),
        (1, 1),
        ((HALF, HALF), (HALF, HALF)),
        dimension_numbers=("NCHW", "OIHW", "NCHW"),
        feature_group_count=channels,
        preferred_element_type=jnp.float32,
    ).reshape(batch, channels, pixels)
    conv = (conv + conv_bias[None, :, None]).astype(jnp.bfloat16)
    values = lax.all_to_all(conv, "swap", split_axis=2, concat_axis=1, tiled=True).astype(
        jnp.float32
    )
    average = jnp.mean(values, axis=1, keepdims=True)
    centred = values - average
    variance = jnp.mean(centred * centred, axis=1, keepdims=True)
    scaled = (
        centred * lax.rsqrt(variance + norm_eps) * norm_gain[None, :, None]
        + norm_shift[None, :, None]
    )
    normed = jnp.swapaxes(scaled, 1, 2).astype(jnp.bfloat16)
    own_rows = normed.reshape(-1, normed.shape[2])
    tokens = lax.all_gather(own_rows, "image", axis=0, tiled=True)
    local_weight = decode(fp8_weight, block_scale)
    weight = lax.all_gather(local_weight, "swap", axis=0, tiled=True)
    frozen = jnp.dot(tokens, weight, preferred_element_type=jnp.float32)
    low_rank = jnp.dot(tokens, adapter_a, preferred_element_type=jnp.float32).astype(jnp.bfloat16)
    pre_act = frozen + adapter_scale * jnp.dot(
        low_rank, adapter_b, preferred_element_type=jnp.float32
    )
    upstream = cotangent.reshape(-1, cotangent.shape[2])
    cumulative = 0.5 * (1.0 + jax.scipy.special.erf(pre_act * 0.7071067811865476))
    slope = cumulative + pre_act * (jnp.exp(-0.5 * pre_act * pre_act) * DENSITY)
    grad_pre = (upstream.astype(jnp.float32) * slope).astype(jnp.bfloat16)
    grad_b = adapter_scale * jnp.dot(low_rank.T, grad_pre, preferred_element_type=jnp.float32)
    back = lax.psum(jnp.dot(grad_pre, adapter_b.T, preferred_element_type=jnp.float32), "image")
    grad_a = adapter_scale * lax.dot_general(
        tokens.astype(jnp.float32),
        back,
        (((0,), (0,)), ((), ())),
        precision=lax.Precision.HIGHEST,
        preferred_element_type=jnp.float32,
    )
    return lax.psum((grad_a, grad_b), "swap")


def solution(mesh):
    placed = (
        P(("group", "image"), "swap", None),
        P("swap", None),
        P("swap"),
        P(),
        P(),
        P("swap", "image"),
        P("swap", "image"),
        P(),
        P(None, "image"),
        P("group", "swap", "image"),
    )
    parts = mesh.shape["swap"]

    def body(*shards):
        _, channels, pixels = shards[0].shape
        span = pixels // parts
        fits = (
            parts <= 8
            and parts & (parts - 1) == 0
            and mesh.shape["image"] == 2
            and channels % 16 == 0
            and span % LANES == 0
            and LANES % W == 0
            and shards[5].shape[1] % LANES == 0
        )
        return functools.partial(shards_kernels, parts)(*shards) if fits else shards_plain(*shards)

    return jax.shard_map(
        body,
        mesh=mesh,
        in_specs=placed,
        out_specs=(P("group", None), P("group", "image")),
        check_vma=False,
    )
```

time: 846 us -> 444 us (0.52)
  Pallas kernels: 0 us -> 255 us
  matrix products: 223 us -> 0 us
  blocking collectives: 190 us -> 0 us
  waiting for transfers between devices: 214 us -> 51.1 us
  local copies, waits for them, and re-layouts: 176 us -> 14.5 us
  starting transfers between devices: 0.16 us -> 102 us
  other arithmetic: 20 us -> 5.09 us
    pallas_call x0 -> x12, Pallas kernels: none -> 255 us  [the longest x4 118 us: conv_image(): pl.pallas_call(functools.partial(conv_body, parts=parts, tile_rows=tile_r...]
    all_to_all x1 -> x0, blocking collectives: 190 us -> none  [shards(): lax.all_to_all(conv, 'swap', split_axis=2, concat_axis=1, tiled=True)]
    all_gather x2 -> x1, waiting for transfers between devices: 134 us -> 0.01 us  [shards_kernels(): weight = lax.all_gather(local_weight, 'swap', axis=0, tiled=True)]
    dot_general x6 -> x0, matrix products: 128 us -> none  [the longest x1 64.7 us: shards(): jnp.dot(columns, shard_rows, preferred_element_type=jnp.float32)]
    ppermute x0 -> x48, starting transfers between devices: none -> 102 us  [the longest x28 75.8 us: shards_kernels(): lax.ppermute(pieces[k], 'swap', across(parts, k))]
    conv_general_dilated x1 -> x0, matrix products: 95.9 us -> none  [depthwise(): lax.conv_general_dilated(maps, taps, (1, 1), ((half_span, half_span), (ha...]
    psum x2 -> x0, waiting for transfers between devices: 79.8 us -> none  [the longest x1 74.4 us: shards(): grad_a, grad_b = lax.psum((grad_a_local, grad_b_local), 'swap')]
    convert_element_type x4 -> x0, local copies, waits for them, and re-layouts: 67.7 us -> none  [the longest x1 31.9 us: shards(): conv = depthwise(images_in, kernel, conv_bias, W).astype(jnp.bfloat16)]
  transfers between devices with their start and end apart: 4 -> 49, of which waited for: 4 -> 11; matrix products, arithmetic and copies ran while one was open for 5% -> 3% of each run, Pallas kernels for 0% -> 51%
where the time goes in v1:
time: 444 us; the launch traced here: 443 us
  Pallas kernels  255 us (57%)
  starting transfers between devices  102 us (23%)
  waiting for transfers between devices  51.1 us (12%)
  between operations  14.9 us (3%)
  local copies, waits for them, and re-layouts  14.5 us (3%)
  other arithmetic  5.09 us (1%)
    pallas_call x4, Pallas kernels, conv_image(): pl.pallas_call(functools.partial(conv_body, parts=parts, tile_rows=tile_r...  118 us
    pallas_call x4, Pallas kernels, main_chunk(): pl.pallas_call(functools.partial(main_body, step=step), grid_spec=pltpu.P...  111 us
    ppermute x28, starting transfers between devices, shards_kernels(): lax.ppermute(pieces[k], 'swap', across(parts, k))  75.8 us
    ppermute x28, waiting for transfers between devices, shards_kernels(): lax.ppermute(pieces[k], 'swap', across(parts, k))  44.6 us
    pallas_call x4, Pallas kernels, norm_image(): pl.pallas_call(functools.partial(norm_body, parts=parts), grid_spec=pltpu...  25.8 us
    ppermute x7, starting transfers between devices, total_over_swap(): piece = lax.ppermute(mine, 'swap', across(parts, k))  12.8 us
    ppermute x7, starting transfers between devices, total_over_swap(): lax.ppermute(lax.dynamic_index_in_dim(share, lax.bitwise_xor(me, k), 0, k...  12.5 us
  transfers between devices with their start and end apart: 49, of which 11 were waited for; matrix products, arithmetic and copies ran while one was open for 3% of the time, Pallas kernels for 51%

profile of v1, /device:TPU:0, one launch (start us, length us, event | category | flops | bytes accessed | tf_op | source)
XLA Modules:
  0.0 443.1 jit_solution(12987012123389664072)
XLA Ops:
  12.7 29.6 %conv_1.1 = (bf16[192,512]{1,0:T(8,128)(2,1)}, bf16[192,512]{1,0:T(8,128)(2,1)}, bf16[192,512]{1,0:T(8,128)(2,1)}, bf16[192,512]{1,0:T(8,128)(2,1)}, bf16[192,51...) custom-call(s32[2]{0:T(128)} %pad_add_fusion.where, ...), custom_call_target="tpu_custom_call" | custom-call | tf_op jit(solution)/shard_map/conv_1/pallas_call | solution.py:109
  42.3 4.0 collective-permute-start.10
  54.0 29.6 %conv_0.1 = (bf16[192,512]{1,0:T(8,128)(2,1)}, bf16[192,512]{1,0:T(8,128)(2,1)}, bf16[192,512]{1,0:T(8,128)(2,1)}, bf16[192,512]{1,0:T(8,128)(2,1)}, bf16[192,51...) custom-call(s32[2]{0:T(128)} %pad_add_fusion.where, ...), custom_call_target="tpu_custom_call" | custom-call | tf_op jit(solution)/shard_map/conv_0/pallas_call | solution.py:109
  84.3 7.0 %collective-permute-done.12.refs_5_ = bf16[192,512]{1,0:T(8,128)(2,1)S(1)} collective-permute-done((bf16[192,512]{1,0:T(8,128)(2,1)}, bf16[192,512]{1,0:T(8,128)(2,1)S(1)}, u32[]{:S(2)}, u32[]{:S(2)}) %collective-permute-start.12) | collective-permute-done | bytes 196640 | tf_op jit(solution)/shard_map/ppermute | solution.py:321
  95.0 10.3 %collective-permute-start.2 = (bf16[192,512]{1,0:T(8,128)(2,1)}, bf16[192,512]{1,0:T(8,128)(2,1)S(1)}, u32[]{:S(2)}, u32[]{:S(2)}) collective-permute-start(bf16[192,512]{1,0:T(8,128)(2,1)} %get-tuple-element.45), channel_id=1, source_target_pairs={{0,6},{2,4},{4,2},{6,0},{8,14},{10,12},{12,10},{14,8},{1,7},{3,5},... | collective-permute-start | bytes 589832 | tf_op jit(solution)/shard_map/ppermute | solution.py:321
  105.3 4.0 collective-permute-start.4
  109.8 29.6 %conv_2.1 = (bf16[192,512]{1,0:T(8,128)(2,1)}, bf16[192,512]{1,0:T(8,128)(2,1)}, bf16[192,512]{1,0:T(8,128)(2,1)}, bf16[192,512]{1,0:T(8,128)(2,1)}, bf16[192,51...) custom-call(s32[2]{0:T(128)} %pad_add_fusion.where, ...), custom_call_target="tpu_custom_call" | custom-call | tf_op jit(solution)/shard_map/conv_2/pallas_call | solution.py:109
  144.4 11.6 %collective-permute-done.4.refs_5_ = bf16[192,512]{1,0:T(8,128)(2,1)S(1)} collective-permute-done((bf16[192,512]{1,0:T(8,128)(2,1)}, bf16[192,512]{1,0:T(8,128)(2,1)S(1)}, u32[]{:S(2)}, u32[]{:S(2)}) %collective-permute-start.4) | collective-permute-done | bytes 196640 | tf_op jit(solution)/shard_map/ppermute | solution.py:321
  156.0 10.1 %collective-permute-start.19 = (bf16[192,512]{1,0:T(8,128)(2,1)}, bf16[192,512]{1,0:T(8,128)(2,1)S(1)}, u32[]{:S(2)}, u32[]{:S(2)}) collective-permute-start(bf16[192,512]{1,0:T(8,128)(2,1)} %get-tuple-element.64), channel_id=1, source_target_pairs={{0,8},{2,10},{4,12},{6,14},{8,0},{10,2},{12,4},{14,6},{1,9},{3,11}... | collective-permute-start | bytes 589832 | tf_op jit(solution)/shard_map/ppermute | solution.py:321
  166.1 29.6 %conv_3.1 = (bf16[192,512]{1,0:T(8,128)(2,1)}, bf16[192,512]{1,0:T(8,128)(2,1)}, bf16[192,512]{1,0:T(8,128)(2,1)}, bf16[192,512]{1,0:T(8,128)(2,1)}, bf16[192,51...) custom-call(s32[2]{0:T(128)} %pad_add_fusion.where, ...), custom_call_target="tpu_custom_call" | custom-call | tf_op jit(solution)/shard_map/conv_3/pallas_call | solution.py:109
  202.6 3.9 collective-permute-done.19.refs_4_
  206.5 22.1 %collective-permute-done.20.refs_5_ = bf16[192,512]{1,0:T(8,128)(2,1)S(1)} collective-permute-done((bf16[192,512]{1,0:T(8,128)(2,1)S(1)}, bf16[192,512]{1,0:T(8,128)(2,1)S(1)}, u32[]{:S(2)}, u32[]{:S(2)}) %collective-permute-start.20) | collective-permute-done | bytes 196640 | tf_op jit(solution)/shard_map/ppermute | solution.py:321
  228.6 6.8 %collective-permute-start.27 = (bf16[192,512]{1,0:T(8,128)(2,1)}, bf16[192,512]{1,0:T(8,128)(2,1)S(1)}, u32[]{:S(2)}, u32[]{:S(2)}) collective-permute-start(bf16[192,512]{1,0:T(8,128)(2,1)} %get-tuple-element.73), channel_id=1, source_target_pairs={{0,8},{2,10},{4,12},{6,14},{8,0},{10,2},{12,4},{14,6},{1,9},{3,11}... | collective-permute-start | bytes 589832 | tf_op jit(solution)/shard_map/ppermute | solution.py:321
  235.4 11.6 %collective-permute-start.28 = (bf16[192,512]{1,0:T(8,128)(2,1)}, bf16[192,512]{1,0:T(8,128)(2,1)S(1)}, u32[]{:S(2)}, u32[]{:S(2)}) collective-permute-start(bf16[192,512]{1,0:T(8,128)(2,1)} %get-tuple-element.74), channel_id=1, source_target_pairs={{0,10},{2,8},{4,14},{6,12},{8,2},{10,0},{12,6},{14,4},{1,11},{3,9}... | collective-permute-start | bytes 589832 | tf_op jit(solution)/shard_map/ppermute | solution.py:321
  254.3 6.4 %norm_1.1.own = bf16[512,1536]{1,0:T(8,128)(2,1)} custom-call(s32[2]{0:T(128)} %pad_add_fusion.where, bf16[192,512]{1,0:T(8,128)(2,1)} %get-tuple-element.51.refs_0_, bf16[192,512]{1,0:T(8,128)(2,1)} %copy-done.12, bf16[192,512]{1,0:T(8,128)(2,1)} %copy-done.13, bf16[192,512]{1,0:T(8,128)(2,1)} %copy-done.7, bf16[192,512]{1,0:T(8,128)(2,1)} %copy-done.8, ...), custom_call_target="tpu_custom_call" | custom-call | tf_op jit(solution)/shard_map/norm_1/pallas_call | solution.py:151
  260.8 6.4 %norm_0.1.own = bf16[512,1536]{1,0:T(8,128)(2,1)} custom-call(s32[2]{0:T(128)} %pad_add_fusion.where, bf16[192,512]{1,0:T(8,128)(2,1)} %get-tuple-element.42.refs_0_, bf16[192,512]{1,0:T(8,128)(2,1)} %copy-done.14, bf16[192,512]{1,0:T(8,128)(2,1)} %copy-done.15, bf16[192,512]{1,0:T(8,128)(2,1)} %copy-done.16, bf16[192,512]{1,0:T(8,128)(2,1)} %copy-done.17, ...), custom_call_target="tpu_custom_call" | custom-call | tf_op jit(solution)/shard_map/norm_0/pallas_call | solution.py:151
  267.1 6.6 %norm_2.1.own = bf16[512,1536]{1,0:T(8,128)(2,1)} custom-call(s32[2]{0:T(128)} %pad_add_fusion.where, bf16[192,512]{1,0:T(8,128)(2,1)} %get-tuple-element.60.refs_0_, bf16[192,512]{1,0:T(8,128)(2,1)} %copy-done.21, bf16[192,512]{1,0:T(8,128)(2,1)} %copy-done.22, bf16[192,512]{1,0:T(8,128)(2,1)} %copy-done.23, bf16[192,512]{1,0:T(8,128)(2,1)} %copy-done.24, ...), custom_call_target="tpu_custom_call" | custom-call | tf_op jit(solution)/shard_map/norm_2/pallas_call | solution.py:151
  275.3 6.5 %norm_3.1.own = bf16[512,1536]{1,0:T(8,128)(2,1)} custom-call(s32[2]{0:T(128)} %pad_add_fusion.where, bf16[192,512]{1,0:T(8,128)(2,1)} %get-tuple-element.69.refs_0_, bf16[192,512]{1,0:T(8,128)(2,1)} %copy-done.25, bf16[192,512]{1,0:T(8,128)(2,1)} %copy-done.26, bf16[192,512]{1,0:T(8,128)(2,1)} %copy-done.28, bf16[192,512]{1,0:T(8,128)(2,1)} %copy-done.30, ...), custom_call_target="tpu_custom_call" | custom-call | tf_op jit(solution)/shard_map/norm_3/pallas_call | solution.py:151
  283.1 27.8 %main_1.1 = (f32[32,1536]{1,0:T(8,128)}, f32[32,3072]{1,0:T(8,128)}) custom-call(s32[2]{0:T(128)} %pad_add_fusion.where, bf16[512,1536]{1,0:T(8,128)(2,1)} %norm_1.1.own, bf16[512,1536]{1,0:T(8,128)(2,1)} %collective-permute-done.15.other, bf16[1536,3072]{1,0:T(8,128)(2,1)} %all-gather.2.cloned.1.call-done.weight, bf16[1536,32]{1,0:T(8,128)(2,1)} %copy.35.down, ...), custom_call_target="tpu_custom_call" | custom-call | tf_op jit(solution)/shard_map/main_1/pallas_call | solution.py:240
  310.9 27.5 %main_0.1 = (f32[32,1536]{1,0:T(8,128)}, f32[32,3072]{1,0:T(8,128)}) custom-call(s32[2]{0:T(128)} %pad_add_fusion.where, bf16[512,1536]{1,0:T(8,128)(2,1)} %norm_0.1.own, bf16[512,1536]{1,0:T(8,128)(2,1)} %collective-permute-done.7.other, bf16[1536,3072]{1,0:T(8,128)(2,1)} %all-gather.2.cloned.1.call-done.weight, bf16[1536,32]{1,0:T(8,128)(2,1)} %copy.35.down, ...), custom_call_target="tpu_custom_call" | custom-call | tf_op jit(solution)/shard_map/main_0/pallas_call | solution.py:240
  338.5 27.9 %main_2.1 = (f32[32,1536]{1,0:T(8,128)}, f32[32,3072]{1,0:T(8,128)}) custom-call(s32[2]{0:T(128)} %pad_add_fusion.where, bf16[512,1536]{1,0:T(8,128)(2,1)} %norm_2.1.own, bf16[512,1536]{1,0:T(8,128)(2,1)} %collective-permute-done.23.other, bf16[1536,3072]{1,0:T(8,128)(2,1)} %all-gather.2.cloned.1.call-done.weight, bf16[1536,32]{1,0:T(8,128)(2,1)} %copy.35.down, ...), custom_call_target="tpu_custom_call" | custom-call | tf_op jit(solution)/shard_map/main_2/pallas_call | solution.py:240
  366.3 27.7 %main_3.1 = (f32[32,1536]{1,0:T(8,128)}, f32[32,3072]{1,0:T(8,128)}) custom-call(s32[2]{0:T(128)} %pad_add_fusion.where, bf16[512,1536]{1,0:T(8,128)(2,1)} %norm_3.1.own, bf16[512,1536]{1,0:T(8,128)(2,1)} %collective-permute-done.31.other, bf16[1536,3072]{1,0:T(8,128)(2,1)} %all-gather.2.cloned.1.call-done.weight, bf16[1536,32]{1,0:T(8,128)(2,1)} %copy.35.down, ...), custom_call_target="tpu_custom_call" | custom-call | tf_op jit(solution)/shard_map/main_3/pallas_call | solution.py:240
  406.4 4.0 collective-permute-start.38
  418.7 3.8 collective-permute-start.43
  (234 shorter events, 74.1 us)
Async XLA Ops:
  7.2 276.0 %all-gather.2.cloned.1.call-start = ((), (), s32[]{:S(2)}) async-start(), calls=%async_computation | async-start | bytes 10616832 | tf_op jit(solution)/shard_map/all_gather | solution.py:315
  42.3 41.3 %collective-permute-start.10 = (bf16[192,512]{1,0:T(8,128)(2,1)}, bf16[192,512]{1,0:T(8,128)(2,1)S(1)}, u32[]{:S(2)}, u32[]{:S(2)}) collective-permute-start(bf16[192,512]{1,0:T(8,128)(2,1)} %get-tuple-element.54), channel_id=1, source_target_pairs={{0,6},{2,4},{4,2},{6,0},{8,14},{10,12},{12,10},{14,8},{1,7},{3,5},... | collective-permute-start | bytes 589832 | tf_op jit(solution)/shard_map/ppermute | solution.py:321
  46.3 37.9 %collective-permute-start.11 = (bf16[192,512]{1,0:T(8,128)(2,1)}, bf16[192,512]{1,0:T(8,128)(2,1)S(1)}, u32[]{:S(2)}, u32[]{:S(2)}) collective-permute-start(bf16[192,512]{1,0:T(8,128)(2,1)} %get-tuple-element.55), channel_id=1, source_target_pairs={{0,8},{2,10},{4,12},{6,14},{8,0},{10,2},{12,4},{14,6},{1,9},{3,11}... | collective-permute-start | bytes 589832 | tf_op jit(solution)/shard_map/ppermute | solution.py:321
  48.9 42.4 %collective-permute-start.12 = (bf16[192,512]{1,0:T(8,128)(2,1)}, bf16[192,512]{1,0:T(8,128)(2,1)S(1)}, u32[]{:S(2)}, u32[]{:S(2)}) collective-permute-start(bf16[192,512]{1,0:T(8,128)(2,1)} %get-tuple-element.56), channel_id=1, source_target_pairs={{0,10},{2,8},{4,14},{6,12},{8,2},{10,0},{12,6},{14,4},{1,11},{3,9}... | collective-permute-start | bytes 589832 | tf_op jit(solution)/shard_map/ppermute | solution.py:321
  49.2 42.4 %collective-permute-start.13 = (bf16[192,512]{1,0:T(8,128)(2,1)}, bf16[192,512]{1,0:T(8,128)(2,1)S(1)}, u32[]{:S(2)}, u32[]{:S(2)}) collective-permute-start(bf16[192,512]{1,0:T(8,128)(2,1)} %get-tuple-element.57), channel_id=1, source_target_pairs={{0,12},{2,14},{4,8},{6,10},{8,4},{10,6},{12,0},{14,2},{1,13},{3,15... | collective-permute-start | bytes 589832 | tf_op jit(solution)/shard_map/ppermute | solution.py:321
  51.7 43.2 %collective-permute-start.14 = (bf16[192,512]{1,0:T(8,128)(2,1)}, bf16[192,512]{1,0:T(8,128)(2,1)S(1)}, u32[]{:S(2)}, u32[]{:S(2)}) collective-permute-start(bf16[192,512]{1,0:T(8,128)(2,1)} %get-tuple-element.58), channel_id=1, source_target_pairs={{0,14},{2,12},{4,10},{6,8},{8,6},{10,4},{12,2},{14,0},{1,15},{3,13... | collective-permute-start | bytes 589832 | tf_op jit(solution)/shard_map/ppermute | solution.py:321
  91.6 47.9 %collective-permute-start.1 = (bf16[192,512]{1,0:T(8,128)(2,1)}, bf16[192,512]{1,0:T(8,128)(2,1)S(1)}, u32[]{:S(2)}, u32[]{:S(2)}) collective-permute-start(bf16[192,512]{1,0:T(8,128)(2,1)} %get-tuple-element.44), channel_id=1, source_target_pairs={{0,4},{2,6},{4,0},{6,2},{8,12},{10,14},{12,8},{14,10},{1,5},{3,7},... | collective-permute-start | bytes 589832 | tf_op jit(solution)/shard_map/ppermute | solution.py:321
  95.0 47.8 %collective-permute-start.2 = (bf16[192,512]{1,0:T(8,128)(2,1)}, bf16[192,512]{1,0:T(8,128)(2,1)S(1)}, u32[]{:S(2)}, u32[]{:S(2)}) collective-permute-start(bf16[192,512]{1,0:T(8,128)(2,1)} %get-tuple-element.45), channel_id=1, source_target_pairs={{0,6},{2,4},{4,2},{6,0},{8,14},{10,12},{12,10},{14,8},{1,7},{3,5},... | collective-permute-start | bytes 589832 | tf_op jit(solution)/shard_map/ppermute | solution.py:321
  105.2 39.1 %collective-permute-start.3 = (bf16[192,512]{1,0:T(8,128)(2,1)}, bf16[192,512]{1,0:T(8,128)(2,1)S(1)}, u32[]{:S(2)}, u32[]{:S(2)}) collective-permute-start(bf16[192,512]{1,0:T(8,128)(2,1)} %get-tuple-element.46), channel_id=1, source_target_pairs={{0,8},{2,10},{4,12},{6,14},{8,0},{10,2},{12,4},{14,6},{1,9},{3,11}... | collective-permute-start | bytes 589832 | tf_op jit(solution)/shard_map/ppermute | solution.py:321
  105.3 50.7 %collective-permute-start.4 = (bf16[192,512]{1,0:T(8,128)(2,1)}, bf16[192,512]{1,0:T(8,128)(2,1)S(1)}, u32[]{:S(2)}, u32[]{:S(2)}) collective-permute-start(bf16[192,512]{1,0:T(8,128)(2,1)} %get-tuple-element.47), channel_id=1, source_target_pairs={{0,10},{2,8},{4,14},{6,12},{8,2},{10,0},{12,6},{14,4},{1,11},{3,9}... | collective-permute-start | bytes 589832 | tf_op jit(solution)/shard_map/ppermute | solution.py:321
  109.2 46.7 %collective-permute-start.5 = (bf16[192,512]{1,0:T(8,128)(2,1)}, bf16[192,512]{1,0:T(8,128)(2,1)S(1)}, u32[]{:S(2)}, u32[]{:S(2)}) collective-permute-start(bf16[192,512]{1,0:T(8,128)(2,1)} %get-tuple-element.48), channel_id=1, source_target_pairs={{0,12},{2,14},{4,8},{6,10},{8,4},{10,6},{12,0},{14,2},{1,13},{3,15... | collective-permute-start | bytes 589832 | tf_op jit(solution)/shard_map/ppermute | solution.py:321
  139.6 56.2 %collective-permute-start.6 = (bf16[192,512]{1,0:T(8,128)(2,1)S(1)}, bf16[192,512]{1,0:T(8,128)(2,1)S(1)}, u32[]{:S(2)}, u32[]{:S(2)}) collective-permute-start(bf16[192,512]{1,0:T(8,128)(2,1)S(1)} %copy-done.43), channel_id=1, source_target_pairs={{0,14},{2,12},{4,10},{6,8},{8,6},{10,4},{12,2},{14,0},{1,15},{3,13... | collective-permute-start | bytes 589832 | tf_op jit(solution)/shard_map/ppermute | solution.py:321
  142.7 54.4 %collective-permute-start.16 = (bf16[192,512]{1,0:T(8,128)(2,1)}, bf16[192,512]{1,0:T(8,128)(2,1)S(1)}, u32[]{:S(2)}, u32[]{:S(2)}) collective-permute-start(bf16[192,512]{1,0:T(8,128)(2,1)} %get-tuple-element.61), channel_id=1, source_target_pairs={{0,2},{2,0},{4,6},{6,4},{8,10},{10,8},{12,14},{14,12},{1,3},{3,1},... | collective-permute-start | bytes 589832 | tf_op jit(solution)/shard_map/ppermute | solution.py:321
  144.4 56.1 %collective-permute-start.17 = (bf16[192,512]{1,0:T(8,128)(2,1)}, bf16[192,512]{1,0:T(8,128)(2,1)S(1)}, u32[]{:S(2)}, u32[]{:S(2)}) collective-permute-start(bf16[192,512]{1,0:T(8,128)(2,1)} %get-tuple-element.62), channel_id=1, source_target_pairs={{0,4},{2,6},{4,0},{6,2},{8,12},{10,14},{12,8},{14,10},{1,5},{3,7},... | collective-permute-start | bytes 589832 | tf_op jit(solution)/shard_map/ppermute | solution.py:321
  155.9 45.1 %collective-permute-start.18 = (bf16[192,512]{1,0:T(8,128)(2,1)}, bf16[192,512]{1,0:T(8,128)(2,1)S(1)}, u32[]{:S(2)}, u32[]{:S(2)}) collective-permute-start(bf16[192,512]{1,0:T(8,128)(2,1)} %get-tuple-element.63), channel_id=1, source_target_pairs={{0,6},{2,4},{4,2},{6,0},{8,14},{10,12},{12,10},{14,8},{1,7},{3,5},... | collective-permute-start | bytes 589832 | tf_op jit(solution)/shard_map/ppermute | solution.py:321
  156.0 50.5 %collective-permute-start.19 = (bf16[192,512]{1,0:T(8,128)(2,1)}, bf16[192,512]{1,0:T(8,128)(2,1)S(1)}, u32[]{:S(2)}, u32[]{:S(2)}) collective-permute-start(bf16[192,512]{1,0:T(8,128)(2,1)} %get-tuple-element.64), channel_id=1, source_target_pairs={{0,8},{2,10},{4,12},{6,14},{8,0},{10,2},{12,4},{14,6},{1,9},{3,11}... | collective-permute-start | bytes 589832 | tf_op jit(solution)/shard_map/ppermute | solution.py:321
  201.0 46.0 %collective-permute-start.24 = (bf16[192,512]{1,0:T(8,128)(2,1)}, bf16[192,512]{1,0:T(8,128)(2,1)S(1)}, u32[]{:S(2)}, u32[]{:S(2)}) collective-permute-start(bf16[192,512]{1,0:T(8,128)(2,1)} %get-tuple-element.70), channel_id=1, source_target_pairs={{0,2},{2,0},{4,6},{6,4},{8,10},{10,8},{12,14},{14,12},{1,3},{3,1},... | collective-permute-start | bytes 589832 | tf_op jit(solution)/shard_map/ppermute | solution.py:321
  206.5 43.5 %collective-permute-start.25 = (bf16[192,512]{1,0:T(8,128)(2,1)}, bf16[192,512]{1,0:T(8,128)(2,1)S(1)}, u32[]{:S(2)}, u32[]{:S(2)}) collective-permute-start(bf16[192,512]{1,0:T(8,128)(2,1)} %get-tuple-element.71), channel_id=1, source_target_pairs={{0,4},{2,6},{4,0},{6,2},{8,12},{10,14},{12,8},{14,10},{1,5},{3,7},... | collective-permute-start | bytes 589832 | tf_op jit(solution)/shard_map/ppermute | solution.py:321
  228.6 45.1 %collective-permute-start.26 = (bf16[192,512]{1,0:T(8,128)(2,1)}, bf16[192,512]{1,0:T(8,128)(2,1)S(1)}, u32[]{:S(2)}, u32[]{:S(2)}) collective-permute-start(bf16[192,512]{1,0:T(8,128)(2,1)} %get-tuple-element.72), channel_id=1, source_target_pairs={{0,6},{2,4},{4,2},{6,0},{8,14},{10,12},{12,10},{14,8},{1,7},{3,5},... | collective-permute-start | bytes 589832 | tf_op jit(solution)/shard_map/ppermute | solution.py:321
  228.6 45.2 %collective-permute-start.27 = (bf16[192,512]{1,0:T(8,128)(2,1)}, bf16[192,512]{1,0:T(8,128)(2,1)S(1)}, u32[]{:S(2)}, u32[]{:S(2)}) collective-permute-start(bf16[192,512]{1,0:T(8,128)(2,1)} %get-tuple-element.73), channel_id=1, source_target_pairs={{0,8},{2,10},{4,12},{6,14},{8,0},{10,2},{12,4},{14,6},{1,9},{3,11}... | collective-permute-start | bytes 589832 | tf_op jit(solution)/shard_map/ppermute | solution.py:321
  235.4 39.0 %collective-permute-start.28 = (bf16[192,512]{1,0:T(8,128)(2,1)}, bf16[192,512]{1,0:T(8,128)(2,1)S(1)}, u32[]{:S(2)}, u32[]{:S(2)}) collective-permute-start(bf16[192,512]{1,0:T(8,128)(2,1)} %get-tuple-element.74), channel_id=1, source_target_pairs={{0,10},{2,8},{4,14},{6,12},{8,2},{10,0},{12,6},{14,4},{1,11},{3,9}... | collective-permute-start | bytes 589832 | tf_op jit(solution)/shard_map/ppermute | solution.py:321
  273.9 37.1 %collective-permute-start.7 = (bf16[512,1536]{1,0:T(8,128)(2,1)S(1)}, bf16[512,1536]{1,0:T(8,128)(2,1)}, u32[]{:S(2)}, u32[]{:S(2)}) collective-permute-start(bf16[512,1536]{1,0:T(8,128)(2,1)S(1)} %copy-done.1), channel_id=1, source_target_pairs={{0,1},{1,0},{2,3},{3,2},{4,5},{5,4},{6,7},{7,6},{8,9},{9,8},{10,11... | collective-permute-start | bytes 4718600 | tf_op jit(solution)/shard_map/ppermute | solution.py:324
  274.4 64.0 %collective-permute-start.23 = (bf16[512,1536]{1,0:T(8,128)(2,1)}, bf16[512,1536]{1,0:T(8,128)(2,1)}, u32[]{:S(2)}, u32[]{:S(2)}) collective-permute-start(bf16[512,1536]{1,0:T(8,128)(2,1)} %norm_2.1.own), channel_id=1, source_target_pairs={{0,1},{1,0},{2,3},{3,2},{4,5},{5,4},{6,7},{7,6},{8,9},{9,8},{10,11... | collective-permute-start | bytes 4718600 | tf_op jit(solution)/shard_map/ppermute | solution.py:324
  281.8 84.5 %collective-permute-start.31 = (bf16[512,1536]{1,0:T(8,128)(2,1)}, bf16[512,1536]{1,0:T(8,128)(2,1)}, u32[]{:S(2)}, u32[]{:S(2)}) collective-permute-start(bf16[512,1536]{1,0:T(8,128)(2,1)} %norm_3.1.own), channel_id=1, source_target_pairs={{0,1},{1,0},{2,3},{3,2},{4,5},{5,4},{6,7},{7,6},{8,9},{9,8},{10,11... | collective-permute-start | bytes 4718600 | tf_op jit(solution)/shard_map/ppermute | solution.py:324
  (74 other events, 1883.5 us)
Sparse Core Ops, SparseCore 0:
  10.7 233.6 all-gather.1
